TPU v7x, 32 devices: a whole 2x2x4 slice. The times are simulated.
32 devices in a mesh: grp: 2 (over x), chan: 16 (over z, y, core).
Axes of the slice: x: 2, y: 2, z: 4, core: 2. Of those that a mesh axis runs over, the one named last changes fastest.
Arguments:
- voltages: bfloat16 [4096, 64, 512], P('chan', 'grp'), parts along dimension 1, may hold values from -6 to 6
- exponents: int32 [64], P('grp'), parts along dimension 0, may hold values from 0 to 2, as said below
- pairs: int32 [128, 2], replicated, may hold values from 0 to 31, as said below
Outputs:
- visibilities: bfloat16 [64, 128, 2, 128, 128], P(('grp', 'chan')), parts along dimension 0
There are 2 independent parts, one for each index of `grp`. A program takes and returns all parts, laid end to end along the dimension named above; an argument that names none is the same for every part. Nothing has to cross between parts.
Inputs may be any that keep to these rules, and one draw needn't show every extreme that they name: exponents are whole numbers. The 128 pairs are distinct and each has first member at most its second.
All inputs are finite; a program needn't handle non-finite values.
Results may differ from a plain program's by a relative error of at most 0.001.
Values may be sent and summed in bfloat16 or wider, within the bound.
A program may use at most 192 MiB of HBM per device.

v0:
```python
import jax
import jax.numpy as jnp
from jax import lax
from jax.sharding import PartitionSpec as P

PANEL = 128
NT = 256


def correlate_plane(plane, pairs):
    width = plane.shape[1]
    half = width // 2
    count = plane.shape[0] // PANEL
    panels = plane.reshape(count, PANEL, width)
    group_size = 32
    groups = pairs.reshape(-1, group_size, 2)
    labels = jnp.arange(count, dtype=jnp.int32)

    def select(which):
        onehot = (which[:, None] == labels[None, :]).astype(jnp.bfloat16)
        picked = jnp.einsum("kn,nix->kix", onehot, panels, preferred_element_type=jnp.float32)
        return picked.astype(jnp.bfloat16).reshape(group_size, PANEL, 2, half)

    def one_group(chosen):
        left = select(chosen[:, 0])
        right = select(chosen[:, 1])
        quads = jnp.einsum("kiat,kjbt->kabij", left, right, preferred_element_type=jnp.float32)
        real_part = quads[:, 0, 0] + quads[:, 1, 1]
        imag_part = quads[:, 1, 0] - quads[:, 0, 1]
        return jnp.stack([real_part, imag_part], axis=1)

    return lax.map(one_group, groups).reshape(-1, 2, PANEL, PANEL)


def correlate_channels(turned, pairs):

    def one_channel(plane):
        return correlate_plane(plane, pairs)

    return lax.map(one_channel, jnp.moveaxis(turned, 1, 0))


def input_power(turned):
    wide = turned.astype(jnp.float32)
    return jnp.sum(wide * wide, axis=(1, 2))


def on_device(voltages, exponents, pairs):
    gain = jnp.exp2(-exponents.astype(jnp.float32)).astype(jnp.bfloat16)
    scaled = voltages * gain[None, :, None]
    total_samples = exponents.shape[0] * NT
    power = lax.all_gather(input_power(scaled), "chan", axis=0, tiled=True)
    turned = lax.all_to_all(scaled, "chan", split_axis=1, concat_axis=0, tiled=True)
    raw = correlate_channels(turned, pairs)
    mean_power = power / total_samples
    rows = mean_power.reshape(-1, PANEL)
    left_power = jnp.take(rows, pairs[:, 0], axis=0)
    right_power = jnp.take(rows, pairs[:, 1], axis=0)
    denom = jnp.sqrt(NT * left_power[:, :, None] * right_power[:, None, :])
    return (raw / denom[None, :, None, :, :]).astype(jnp.bfloat16)


def solution(mesh):
    return jax.shard_map(
        on_device,
        mesh=mesh,
        in_specs=(P("chan", "grp", None), P("grp"), P()),
        out_specs=P(("grp", "chan"), None, None, None, None),
        check_vma=False,
    )
```

profile of v0, /device:TPU:11, one launch (start us, length us, event | category | flops | bytes accessed | tf_op | source)
XLA Modules:
  0.0 683.6 jit_solution(13939410700513925443)
XLA Ops:
  0.7 9.6 %multiply_reduce_fusion = (f32[256]{0:T(256)S(1)}, bf16[256,32,512]{2,0,1:T(8,128)(2,1)}) fusion(bf16[32]{0:T(256)(128)(2,1)S(1)} %exponential_convert_fusion, bf16[256,32,512]{2,1,0:T(8,128)(2,1)} %param.9), kind=kLoop, calls=%fused_computation.29 | loop fusion | flops 16776960 | bytes 16778304 | tf_op jit(solution)/shard_map/reduce_sum | solution.py:45
  10.3 6.7 all-to-all-start
  17.1 192.6 %all-gather = f32[16,1,256]{2,1,0:T(1,128)S(1)} all-gather(f32[1,1,256]{2,1,0:T(1,128)S(1)} %bitcast.99), channel_id=1, replica_groups=mesh['grp'=2,'chan'=16] {'chan'}, dimensions={0}, use_global_device_ids=true | all-gather | bytes 17408 | tf_op jit(solution)/shard_map/all_gather | solution.py:52
  215.7 7.5 %copy.26 = bf16[16,256,2,512]{3,1,0,2:T(8,128)(2,1)} copy(bf16[16,256,2,512]{3,1,2,0:T(8,128)(2,1)} %bitcast.3) | data formatting | bytes 16777216 | tf_op jit(solution)/shard_map/all_to_all | solution.py:53
  223.2 440.5 %while.23 = (s32[]{:T(128)}, f32[2,128,2,128,128]{4,3,2,1,0:T(8,128)}, s32[128,2]{0,1:T(2,128)S(1)}, bf16[2,4096,512]{2,1,0:T(8,128)(2,1)}, s32[]{:T(128)}, /*index=5*/s32[]{:T(128)}, s32[]{:T(128)}) while((s32[]{:T(128)}, f32[2,128,2,128,128]{4,3,2,1,0:T(8,128)}, s32[128,2]{0,1:T(2,128)S(1)}, bf16[2,4096,512]{2,1,0:T(8,128)(2,1)}, s32[]{:T(128)}, ...), condition=%wide.region_3.4_spmd, body=%wide.region_0.3_spmd.sunk | while | flops 1348470784 | bytes 138415600 | solution.py:40
  230.2 201.7 %while.24 = (s32[]{:T(128)}, f32[4,32,2,128,128]{4,3,2,1,0:T(8,128)}, s32[4,32,2]{1,0,2:T(4,128)S(1)}, bf16[32,128,512]{2,0,1:T(8,128)(2,1)}, s32[]{:T(128)}) while((s32[]{:T(128)}, f32[4,32,2,128,128]{4,3,2,1,0:T(8,128)}, s32[4,32,2]{1,0,2:T(4,128)S(1)}, bf16[32,128,512]{2,0,1:T(8,128)(2,1)}, s32[]{:T(128)}) %tuple.52), condition=%wide.region_2.2_spmd.clone.clone, body=%wide.region_1.1_spmd.clone.clone.sunk | while | flops 1348470784 | bytes 88081744 | solution.py:32
  230.2 5.4 convolution_convert_fusion.4
  235.6 6.9 %reshape.106 = bf16[32,128,2,256]{3,2,0,1:T(2,128)(2,1)} reshape(bf16[32,128,512]{2,0,1:T(8,128)(2,1)} %convolution_convert_fusion.4) | data formatting | bytes 8388608 | tf_op jit(solution)/shard_map/while/body/eval_jaxpr/while/body/eval_jaxpr/reshape | solution.py:22
  242.6 5.4 convolution_convert_fusion.5
  248.0 6.9 %reshape.107 = bf16[32,128,2,256]{3,2,0,1:T(2,128)(2,1)} reshape(bf16[32,128,512]{2,0,1:T(8,128)(2,1)} %convolution_convert_fusion.5) | data formatting | bytes 8388608 | tf_op jit(solution)/shard_map/while/body/eval_jaxpr/while/body/eval_jaxpr/reshape | solution.py:22
  254.9 12.5 %fusion.36 = f32[32,2,2,128,128]{3,4,1,2,0:T(8,128)S(1)} fusion(bf16[32,128,2,256,1]{3,2,0,1,4:T(2,128)(2,1)} %bitcast.91, bf16[32,128,2,256,1]{3,2,0,1,4:T(2,128)(2,1)} %bitcast.92), kind=kOutput, calls=%fused_computation.7.clone.1 | convolution fusion | flops 1073741824 | bytes 16777216 | tf_op jit(solution)/shard_map/while/body/eval_jaxpr/while/body/eval_jaxpr/kiat,kjbt->kabij/dot_general | solution.py:27
  270.3 5.6 copy.55
  275.9 4.7 constant_dynamic-update-slice_fusion.2
  280.6 5.4 convolution_convert_fusion.4
  286.0 6.9 %reshape.106 = bf16[32,128,2,256]{3,2,0,1:T(2,128)(2,1)} reshape(bf16[32,128,512]{2,0,1:T(8,128)(2,1)} %convolution_convert_fusion.4) | data formatting | bytes 8388608 | tf_op jit(solution)/shard_map/while/body/eval_jaxpr/while/body/eval_jaxpr/reshape | solution.py:22
  293.0 5.4 convolution_convert_fusion.5
  298.4 6.9 %reshape.107 = bf16[32,128,2,256]{3,2,0,1:T(2,128)(2,1)} reshape(bf16[32,128,512]{2,0,1:T(8,128)(2,1)} %convolution_convert_fusion.5) | data formatting | bytes 8388608 | tf_op jit(solution)/shard_map/while/body/eval_jaxpr/while/body/eval_jaxpr/reshape | solution.py:22
  305.3 12.5 %fusion.36 = f32[32,2,2,128,128]{3,4,1,2,0:T(8,128)S(1)} fusion(bf16[32,128,2,256,1]{3,2,0,1,4:T(2,128)(2,1)} %bitcast.91, bf16[32,128,2,256,1]{3,2,0,1,4:T(2,128)(2,1)} %bitcast.92), kind=kOutput, calls=%fused_computation.7.clone.1 | convolution fusion | flops 1073741824 | bytes 16777216 | tf_op jit(solution)/shard_map/while/body/eval_jaxpr/while/body/eval_jaxpr/kiat,kjbt->kabij/dot_general | solution.py:27
  320.7 5.6 copy.55
  326.3 4.7 constant_dynamic-update-slice_fusion.2
  331.0 5.4 convolution_convert_fusion.4
  336.4 6.9 %reshape.106 = bf16[32,128,2,256]{3,2,0,1:T(2,128)(2,1)} reshape(bf16[32,128,512]{2,0,1:T(8,128)(2,1)} %convolution_convert_fusion.4) | data formatting | bytes 8388608 | tf_op jit(solution)/shard_map/while/body/eval_jaxpr/while/body/eval_jaxpr/reshape | solution.py:22
  343.4 5.4 convolution_convert_fusion.5
  348.8 6.9 %reshape.107 = bf16[32,128,2,256]{3,2,0,1:T(2,128)(2,1)} reshape(bf16[32,128,512]{2,0,1:T(8,128)(2,1)} %convolution_convert_fusion.5) | data formatting | bytes 8388608 | tf_op jit(solution)/shard_map/while/body/eval_jaxpr/while/body/eval_jaxpr/reshape | solution.py:22
  355.7 12.5 %fusion.36 = f32[32,2,2,128,128]{3,4,1,2,0:T(8,128)S(1)} fusion(bf16[32,128,2,256,1]{3,2,0,1,4:T(2,128)(2,1)} %bitcast.91, bf16[32,128,2,256,1]{3,2,0,1,4:T(2,128)(2,1)} %bitcast.92), kind=kOutput, calls=%fused_computation.7.clone.1 | convolution fusion | flops 1073741824 | bytes 16777216 | tf_op jit(solution)/shard_map/while/body/eval_jaxpr/while/body/eval_jaxpr/kiat,kjbt->kabij/dot_general | solution.py:27
  371.1 5.6 copy.55
  381.4 5.4 convolution_convert_fusion.4
  386.9 6.9 %reshape.106 = bf16[32,128,2,256]{3,2,0,1:T(2,128)(2,1)} reshape(bf16[32,128,512]{2,0,1:T(8,128)(2,1)} %convolution_convert_fusion.4) | data formatting | bytes 8388608 | tf_op jit(solution)/shard_map/while/body/eval_jaxpr/while/body/eval_jaxpr/reshape | solution.py:22
  393.8 5.4 convolution_convert_fusion.5
  399.2 6.9 %reshape.107 = bf16[32,128,2,256]{3,2,0,1:T(2,128)(2,1)} reshape(bf16[32,128,512]{2,0,1:T(8,128)(2,1)} %convolution_convert_fusion.5) | data formatting | bytes 8388608 | tf_op jit(solution)/shard_map/while/body/eval_jaxpr/while/body/eval_jaxpr/reshape | solution.py:22
  406.1 12.5 %fusion.36 = f32[32,2,2,128,128]{3,4,1,2,0:T(8,128)S(1)} fusion(bf16[32,128,2,256,1]{3,2,0,1,4:T(2,128)(2,1)} %bitcast.91, bf16[32,128,2,256,1]{3,2,0,1,4:T(2,128)(2,1)} %bitcast.92), kind=kOutput, calls=%fused_computation.7.clone.1 | convolution fusion | flops 1073741824 | bytes 16777216 | tf_op jit(solution)/shard_map/while/body/eval_jaxpr/while/body/eval_jaxpr/kiat,kjbt->kabij/dot_general | solution.py:27
  421.5 5.6 copy.55
  431.8 11.6 %bitcast_dynamic-update-slice_fusion.2 = f32[2,128,2,128,128]{4,3,2,1,0:T(8,128)} fusion(f32[2,128,2,128,128]{4,3,2,1,0:T(8,128)} %get-tuple-element.207, s32[]{:T(128)S(6)} %copy.66, f32[1,128,2,128,128]{4,3,2,1,0:T(8,128)} %bitcast.93), kind=kLoop, calls=%fused_computation.26.clone.1 | loop fusion | bytes 33554436 | tf_op jit(solution)/shard_map/while/body/jit(dynamic_update_index_in_dim)/dynamic_update_slice | solution.py:40
  450.5 201.6 %while.24 = (s32[]{:T(128)}, f32[4,32,2,128,128]{4,3,2,1,0:T(8,128)}, s32[4,32,2]{1,0,2:T(4,128)S(1)}, bf16[32,128,512]{2,0,1:T(8,128)(2,1)}, s32[]{:T(128)}) while((s32[]{:T(128)}, f32[4,32,2,128,128]{4,3,2,1,0:T(8,128)}, s32[4,32,2]{1,0,2:T(4,128)S(1)}, bf16[32,128,512]{2,0,1:T(8,128)(2,1)}, s32[]{:T(128)}) %tuple.52), condition=%wide.region_2.2_spmd.clone.clone, body=%wide.region_1.1_spmd.clone.clone.sunk | while | flops 1348470784 | bytes 88081744 | solution.py:32
  450.5 5.4 convolution_convert_fusion.4
  455.9 6.9 %reshape.106 = bf16[32,128,2,256]{3,2,0,1:T(2,128)(2,1)} reshape(bf16[32,128,512]{2,0,1:T(8,128)(2,1)} %convolution_convert_fusion.4) | data formatting | bytes 8388608 | tf_op jit(solution)/shard_map/while/body/eval_jaxpr/while/body/eval_jaxpr/reshape | solution.py:22
  462.8 5.4 convolution_convert_fusion.5
  468.3 6.9 %reshape.107 = bf16[32,128,2,256]{3,2,0,1:T(2,128)(2,1)} reshape(bf16[32,128,512]{2,0,1:T(8,128)(2,1)} %convolution_convert_fusion.5) | data formatting | bytes 8388608 | tf_op jit(solution)/shard_map/while/body/eval_jaxpr/while/body/eval_jaxpr/reshape | solution.py:22
  475.1 12.5 %fusion.36 = f32[32,2,2,128,128]{3,4,1,2,0:T(8,128)S(1)} fusion(bf16[32,128,2,256,1]{3,2,0,1,4:T(2,128)(2,1)} %bitcast.91, bf16[32,128,2,256,1]{3,2,0,1,4:T(2,128)(2,1)} %bitcast.92), kind=kOutput, calls=%fused_computation.7.clone.1 | convolution fusion | flops 1073741824 | bytes 16777216 | tf_op jit(solution)/shard_map/while/body/eval_jaxpr/while/body/eval_jaxpr/kiat,kjbt->kabij/dot_general | solution.py:27
  490.5 5.6 copy.55
  496.2 4.7 constant_dynamic-update-slice_fusion.2
  500.9 5.4 convolution_convert_fusion.4
  506.3 6.9 %reshape.106 = bf16[32,128,2,256]{3,2,0,1:T(2,128)(2,1)} reshape(bf16[32,128,512]{2,0,1:T(8,128)(2,1)} %convolution_convert_fusion.4) | data formatting | bytes 8388608 | tf_op jit(solution)/shard_map/while/body/eval_jaxpr/while/body/eval_jaxpr/reshape | solution.py:22
  513.2 5.4 convolution_convert_fusion.5
  518.7 6.9 %reshape.107 = bf16[32,128,2,256]{3,2,0,1:T(2,128)(2,1)} reshape(bf16[32,128,512]{2,0,1:T(8,128)(2,1)} %convolution_convert_fusion.5) | data formatting | bytes 8388608 | tf_op jit(solution)/shard_map/while/body/eval_jaxpr/while/body/eval_jaxpr/reshape | solution.py:22
  525.5 12.5 %fusion.36 = f32[32,2,2,128,128]{3,4,1,2,0:T(8,128)S(1)} fusion(bf16[32,128,2,256,1]{3,2,0,1,4:T(2,128)(2,1)} %bitcast.91, bf16[32,128,2,256,1]{3,2,0,1,4:T(2,128)(2,1)} %bitcast.92), kind=kOutput, calls=%fused_computation.7.clone.1 | convolution fusion | flops 1073741824 | bytes 16777216 | tf_op jit(solution)/shard_map/while/body/eval_jaxpr/while/body/eval_jaxpr/kiat,kjbt->kabij/dot_general | solution.py:27
  540.9 5.6 copy.55
  546.6 4.7 constant_dynamic-update-slice_fusion.2
  551.3 5.4 convolution_convert_fusion.4
  556.7 6.9 %reshape.106 = bf16[32,128,2,256]{3,2,0,1:T(2,128)(2,1)} reshape(bf16[32,128,512]{2,0,1:T(8,128)(2,1)} %convolution_convert_fusion.4) | data formatting | bytes 8388608 | tf_op jit(solution)/shard_map/while/body/eval_jaxpr/while/body/eval_jaxpr/reshape | solution.py:22
  563.6 5.4 convolution_convert_fusion.5
  569.1 6.9 %reshape.107 = bf16[32,128,2,256]{3,2,0,1:T(2,128)(2,1)} reshape(bf16[32,128,512]{2,0,1:T(8,128)(2,1)} %convolution_convert_fusion.5) | data formatting | bytes 8388608 | tf_op jit(solution)/shard_map/while/body/eval_jaxpr/while/body/eval_jaxpr/reshape | solution.py:22
  575.9 12.5 %fusion.36 = f32[32,2,2,128,128]{3,4,1,2,0:T(8,128)S(1)} fusion(bf16[32,128,2,256,1]{3,2,0,1,4:T(2,128)(2,1)} %bitcast.91, bf16[32,128,2,256,1]{3,2,0,1,4:T(2,128)(2,1)} %bitcast.92), kind=kOutput, calls=%fused_computation.7.clone.1 | convolution fusion | flops 1073741824 | bytes 16777216 | tf_op jit(solution)/shard_map/while/body/eval_jaxpr/while/body/eval_jaxpr/kiat,kjbt->kabij/dot_general | solution.py:27
  591.3 5.6 copy.55
  597.0 4.7 constant_dynamic-update-slice_fusion.2
  601.7 5.4 convolution_convert_fusion.4
  607.1 6.9 %reshape.106 = bf16[32,128,2,256]{3,2,0,1:T(2,128)(2,1)} reshape(bf16[32,128,512]{2,0,1:T(8,128)(2,1)} %convolution_convert_fusion.4) | data formatting | bytes 8388608 | tf_op jit(solution)/shard_map/while/body/eval_jaxpr/while/body/eval_jaxpr/reshape | solution.py:22
  614.0 5.4 convolution_convert_fusion.5
  619.5 6.9 %reshape.107 = bf16[32,128,2,256]{3,2,0,1:T(2,128)(2,1)} reshape(bf16[32,128,512]{2,0,1:T(8,128)(2,1)} %convolution_convert_fusion.5) | data formatting | bytes 8388608 | tf_op jit(solution)/shard_map/while/body/eval_jaxpr/while/body/eval_jaxpr/reshape | solution.py:22
  626.3 12.5 %fusion.36 = f32[32,2,2,128,128]{3,4,1,2,0:T(8,128)S(1)} fusion(bf16[32,128,2,256,1]{3,2,0,1,4:T(2,128)(2,1)} %bitcast.91, bf16[32,128,2,256,1]{3,2,0,1,4:T(2,128)(2,1)} %bitcast.92), kind=kOutput, calls=%fused_computation.7.clone.1 | convolution fusion | flops 1073741824 | bytes 16777216 | tf_op jit(solution)/shard_map/while/body/eval_jaxpr/while/body/eval_jaxpr/kiat,kjbt->kabij/dot_general | solution.py:27
  641.7 5.6 copy.55
  647.4 4.7 constant_dynamic-update-slice_fusion.2
  652.1 11.6 %bitcast_dynamic-update-slice_fusion.2 = f32[2,128,2,128,128]{4,3,2,1,0:T(8,128)} fusion(f32[2,128,2,128,128]{4,3,2,1,0:T(8,128)} %get-tuple-element.207, s32[]{:T(128)S(6)} %copy.66, f32[1,128,2,128,128]{4,3,2,1,0:T(8,128)} %bitcast.93), kind=kLoop, calls=%fused_computation.26.clone.1 | loop fusion | bytes 33554436 | tf_op jit(solution)/shard_map/while/body/jit(dynamic_update_index_in_dim)/dynamic_update_slice | solution.py:40
  663.7 19.9 %divide_convert_fusion = bf16[2,128,2,128,128]{4,3,2,1,0:T(8,128)(2,1)} fusion(f32[2,128,2,128,128]{4,3,2,1,0:T(8,128)} %get-tuple-element.58, f32[128,128,128]{2,1,0:T(8,128)} %multiply_sqrt_fusion), kind=kLoop, calls=%fused_computation.28 | loop fusion | flops 16777216 | bytes 58720256 | tf_op jit(solution)/shard_map/convert_element_type | solution.py:60
  (63 shorter events, 53.1 us)
Async XLA Ops:
  10.3 199.4 %copy-start = (s32[128,2]{0,1:T(2,128)S(1)}, s32[128,2]{0,1:T(2,128)}, u32[]{:S(2)}) copy-start(s32[128,2]{0,1:T(2,128)} %param.11) | copy-start | bytes 3076
  10.3 205.4 %all-to-all-start = ((bf16[256,32,512]{2,0,1:T(8,128)(2,1)}), bf16[256,32,512]{2,0,1:T(8,128)(2,1)}, u32[]{:S(2)}, u32[]{:S(2)}) async-start(bf16[256,32,512]{2,0,1:T(8,128)(2,1)} %get-tuple-element.112), calls=%async_computation | async-start | bytes 16777216 | tf_op jit(solution)/shard_map/all_to_all | solution.py:53
where the time goes:
time: 688 us; the launch traced here: 684 us
  local copies, waits for them, and re-layouts  239 us (35%)
  blocking collectives  193 us (28%)
  matrix products  187 us (27%)
  other arithmetic  57.9 us (8%)
    all_gather x1, blocking collectives, on_device(): power = lax.all_gather(input_power(scaled), 'chan', axis=0, tiled=True)  193 us
    reshape x16, local copies, waits for them, and re-layouts, select(): return picked.astype(jnp.bfloat16).reshape(group_size, PANEL, 2, half)  111 us
    dot_general x8, matrix products, one_group(): jnp.einsum('kiat,kjbt->kabij', left, right, preferred_element_type=jnp.fl...  100 us
    dot_general x16, matrix products, select(): jnp.einsum('kn,nix->kix', onehot, panels, preferred_element_type=jnp.floa...  86.8 us
    dynamic_update_slice x16, local copies, waits for them, and re-layouts, correlate_plane(): return lax.map(one_group, groups).reshape(-1, 2, PANEL, PANEL)  82.5 us
    dynamic_update_slice x2, local copies, waits for them, and re-layouts, correlate_channels(): return lax.map(one_channel, jnp.moveaxis(turned, 1, 0))  23.3 us
    convert_element_type x1, other arithmetic, on_device(): return (raw / denom[None, :, None, :, :]).astype(jnp.bfloat16)  19.9 us
    broadcast_in_dim x8, other arithmetic, correlate_plane(): return lax.map(one_group, groups).reshape(-1, 2, PANEL, PANEL)  18 us
  transfers between devices with their start and end apart: 1, of which 0 were waited for; matrix products, arithmetic and copies ran while one was open for 1% of the time, Pallas kernels for 0%

commit v1 on v0

--- a/solution.py
+++ b/solution.py
@@ -50,7 +50,16 @@
     scaled = voltages * gain[None, :, None]
     total_samples = exponents.shape[0] * NT
     power = lax.all_gather(input_power(scaled), "chan", axis=0, tiled=True)
-    turned = lax.all_to_all(scaled, "chan", split_axis=1, concat_axis=0, tiled=True)
+    _derive_entries = lambda pos_dim, axis_k, vec: jnp.concatenate(
+        lax.all_to_all(
+            jnp.stack(jnp.split(vec, lax.axis_size("chan"), axis_k), 0),
+            split_axis=0,
+            concat_axis=0,
+            axis_name="chan",
+        ),
+        pos_dim,
+    )
+    turned = _derive_entries(0, 1, scaled)
     raw = correlate_channels(turned, pairs)
     mean_power = power / total_samples
     rows = mean_power.reshape(-1, PANEL)

time: 688 us -> 723 us (1.051)
  local copies, waits for them, and re-layouts: 239 us -> 275 us
    unnamed x2 -> x19, local copies, waits for them, and re-layouts: 0.01 us -> 33.1 us
where the time goes in v1:
time: 723 us; the launch traced here: 719 us
  local copies, waits for them, and re-layouts  275 us (38%)
  blocking collectives  193 us (27%)
  matrix products  187 us (26%)
  other arithmetic  57.8 us (8%)
    all_gather x1, blocking collectives, on_device(): power = lax.all_gather(input_power(scaled), 'chan', axis=0, tiled=True)  193 us
    reshape x16, local copies, waits for them, and re-layouts, select(): return picked.astype(jnp.bfloat16).reshape(group_size, PANEL, 2, half)  111 us
    dot_general x8, matrix products, one_group(): jnp.einsum('kiat,kjbt->kabij', left, right, preferred_element_type=jnp.fl...  100 us
    dot_general x16, matrix products, select(): jnp.einsum('kn,nix->kix', onehot, panels, preferred_element_type=jnp.floa...  86.7 us
    dynamic_update_slice x16, local copies, waits for them, and re-layouts, correlate_plane(): return lax.map(one_group, groups).reshape(-1, 2, PANEL, PANEL)  82.4 us
    unnamed x19, local copies, waits for them, and re-layouts  33.1 us
    dynamic_update_slice x2, local copies, waits for them, and re-layouts, correlate_channels(): return lax.map(one_channel, jnp.moveaxis(turned, 1, 0))  23.3 us
    convert_element_type x1, other arithmetic, on_device(): return (raw / denom[None, :, None, :, :]).astype(jnp.bfloat16)  19.9 us
  transfers between devices with their start and end apart: 1, of which 0 were waited for; matrix products, arithmetic and copies ran while one was open for 1% of the time, Pallas kernels for 0%

profile of v1, /device:TPU:11, one launch (start us, length us, event | category | flops | bytes accessed | tf_op | source)
XLA Modules:
  0.0 718.9 jit_solution(2065897885350902417)
XLA Ops:
  0.7 9.5 %multiply_reduce_fusion = (f32[256]{0:T(256)S(1)}, bf16[256,32,512]{2,1,0:T(8,128)(2,1)}) fusion(bf16[256,32,512]{2,1,0:T(8,128)(2,1)} %param.9, bf16[32]{0:T(256)(128)(2,1)S(1)} %exponential_convert_fusion), kind=kLoop, calls=%fused_computation.29 | loop fusion | flops 16776960 | bytes 16778304 | tf_op jit(solution)/shard_map/reduce_sum | solution.py:45
  44.7 6.9 all-to-all-start
  51.6 192.6 %all-gather = f32[16,1,256]{2,1,0:T(1,128)S(1)} all-gather(f32[1,1,256]{2,1,0:T(1,128)S(1)} %bitcast.160), channel_id=1, replica_groups=mesh['grp'=2,'chan'=16] {'chan'}, dimensions={0}, use_global_device_ids=true | all-gather | bytes 17408 | tf_op jit(solution)/shard_map/all_gather | solution.py:52
  250.3 8.5 %copy.25 = bf16[16,256,2,512]{3,1,0,2:T(8,128)(2,1)} copy(bf16[16,256,2,512]{3,2,1,0:T(2,128)(2,1)} %all-to-all-done) | data formatting | bytes 16777216 | tf_op jit(solution)/shard_map/all_to_all | solution.py:54
  258.8 440.2 %while.23 = (s32[]{:T(128)}, f32[2,128,2,128,128]{4,3,2,1,0:T(8,128)}, s32[128,2]{0,1:T(2,128)S(1)}, bf16[2,4096,512]{2,1,0:T(8,128)(2,1)}, s32[]{:T(128)}, /*index=5*/s32[]{:T(128)}, s32[]{:T(128)}) while((s32[]{:T(128)}, f32[2,128,2,128,128]{4,3,2,1,0:T(8,128)}, s32[128,2]{0,1:T(2,128)S(1)}, bf16[2,4096,512]{2,1,0:T(8,128)(2,1)}, s32[]{:T(128)}, ...), condition=%wide.region_3.4_spmd, body=%wide.region_0.3_spmd.sunk | while | flops 1348470784 | bytes 138416592 | solution.py:40
  265.7 201.5 %while.24 = (s32[]{:T(128)}, f32[4,32,2,128,128]{4,3,2,1,0:T(8,128)}, s32[4,32,2]{1,0,2:T(4,128)S(1)}, bf16[32,128,512]{2,0,1:T(8,128)(2,1)}, s32[]{:T(128)}) while((s32[]{:T(128)}, f32[4,32,2,128,128]{4,3,2,1,0:T(8,128)}, s32[4,32,2]{1,0,2:T(4,128)S(1)}, bf16[32,128,512]{2,0,1:T(8,128)(2,1)}, s32[]{:T(128)}) %tuple.52), condition=%wide.region_2.2_spmd.clone.clone, body=%wide.region_1.1_spmd.clone.clone.sunk | while | flops 1348470784 | bytes 88082240 | solution.py:32
  265.8 5.4 convolution_convert_fusion.4
  271.2 6.9 reshape.110
  278.1 5.4 convolution_convert_fusion.5
  283.6 6.9 reshape.111
  290.5 12.5 %fusion.52 = f32[32,2,2,128,128]{3,4,1,2,0:T(8,128)S(1)} fusion(bf16[32,128,2,256,1]{3,2,0,1,4:T(2,128)(2,1)} %bitcast.152, bf16[32,128,2,256,1]{3,2,0,1,4:T(2,128)(2,1)} %bitcast.153), kind=kOutput, calls=%fused_computation.7.clone.1 | convolution fusion | flops 1073741824 | bytes 16777216 | tf_op jit(solution)/shard_map/while/body/eval_jaxpr/while/body/eval_jaxpr/kiat,kjbt->kabij/dot_general | solution.py:27
  305.8 5.6 copy.52
  311.4 4.7 constant_dynamic-update-slice_fusion.2
  316.2 5.4 convolution_convert_fusion.4
  321.6 6.9 reshape.110
  328.5 5.4 convolution_convert_fusion.5
  333.9 6.9 reshape.111
  340.8 12.5 %fusion.52 = f32[32,2,2,128,128]{3,4,1,2,0:T(8,128)S(1)} fusion(bf16[32,128,2,256,1]{3,2,0,1,4:T(2,128)(2,1)} %bitcast.152, bf16[32,128,2,256,1]{3,2,0,1,4:T(2,128)(2,1)} %bitcast.153), kind=kOutput, calls=%fused_computation.7.clone.1 | convolution fusion | flops 1073741824 | bytes 16777216 | tf_op jit(solution)/shard_map/while/body/eval_jaxpr/while/body/eval_jaxpr/kiat,kjbt->kabij/dot_general | solution.py:27
  356.2 5.6 copy.52
  361.8 4.7 constant_dynamic-update-slice_fusion.2
  366.5 5.4 convolution_convert_fusion.4
  371.9 6.9 reshape.110
  378.9 5.4 convolution_convert_fusion.5
  384.3 6.9 reshape.111
  391.2 12.5 %fusion.52 = f32[32,2,2,128,128]{3,4,1,2,0:T(8,128)S(1)} fusion(bf16[32,128,2,256,1]{3,2,0,1,4:T(2,128)(2,1)} %bitcast.152, bf16[32,128,2,256,1]{3,2,0,1,4:T(2,128)(2,1)} %bitcast.153), kind=kOutput, calls=%fused_computation.7.clone.1 | convolution fusion | flops 1073741824 | bytes 16777216 | tf_op jit(solution)/shard_map/while/body/eval_jaxpr/while/body/eval_jaxpr/kiat,kjbt->kabij/dot_general | solution.py:27
  406.6 5.6 copy.52
  412.2 4.7 constant_dynamic-update-slice_fusion.2
  416.9 5.4 convolution_convert_fusion.4
  422.3 6.9 reshape.110
  429.3 5.4 convolution_convert_fusion.5
  434.7 6.9 reshape.111
  441.6 12.5 %fusion.52 = f32[32,2,2,128,128]{3,4,1,2,0:T(8,128)S(1)} fusion(bf16[32,128,2,256,1]{3,2,0,1,4:T(2,128)(2,1)} %bitcast.152, bf16[32,128,2,256,1]{3,2,0,1,4:T(2,128)(2,1)} %bitcast.153), kind=kOutput, calls=%fused_computation.7.clone.1 | convolution fusion | flops 1073741824 | bytes 16777216 | tf_op jit(solution)/shard_map/while/body/eval_jaxpr/while/body/eval_jaxpr/kiat,kjbt->kabij/dot_general | solution.py:27
  457.0 5.6 copy.52
  462.6 4.7 constant_dynamic-update-slice_fusion.2
  467.3 11.6 %bitcast_dynamic-update-slice_fusion.2 = f32[2,128,2,128,128]{4,3,2,1,0:T(8,128)} fusion(f32[2,128,2,128,128]{4,3,2,1,0:T(8,128)} %get-tuple-element.207, s32[]{:T(128)} %get-tuple-element.206, f32[1,128,2,128,128]{4,3,2,1,0:T(8,128)} %bitcast.154), kind=kLoop, calls=%fused_computation.26.clone.1 | loop fusion | bytes 33554944 | tf_op jit(solution)/shard_map/while/body/jit(dynamic_update_index_in_dim)/dynamic_update_slice | solution.py:40
  485.9 201.5 %while.24 = (s32[]{:T(128)}, f32[4,32,2,128,128]{4,3,2,1,0:T(8,128)}, s32[4,32,2]{1,0,2:T(4,128)S(1)}, bf16[32,128,512]{2,0,1:T(8,128)(2,1)}, s32[]{:T(128)}) while((s32[]{:T(128)}, f32[4,32,2,128,128]{4,3,2,1,0:T(8,128)}, s32[4,32,2]{1,0,2:T(4,128)S(1)}, bf16[32,128,512]{2,0,1:T(8,128)(2,1)}, s32[]{:T(128)}) %tuple.52), condition=%wide.region_2.2_spmd.clone.clone, body=%wide.region_1.1_spmd.clone.clone.sunk | while | flops 1348470784 | bytes 88082240 | solution.py:32
  485.9 5.4 convolution_convert_fusion.4
  491.3 6.9 reshape.110
  498.2 5.4 convolution_convert_fusion.5
  503.7 6.9 reshape.111
  510.6 12.5 %fusion.52 = f32[32,2,2,128,128]{3,4,1,2,0:T(8,128)S(1)} fusion(bf16[32,128,2,256,1]{3,2,0,1,4:T(2,128)(2,1)} %bitcast.152, bf16[32,128,2,256,1]{3,2,0,1,4:T(2,128)(2,1)} %bitcast.153), kind=kOutput, calls=%fused_computation.7.clone.1 | convolution fusion | flops 1073741824 | bytes 16777216 | tf_op jit(solution)/shard_map/while/body/eval_jaxpr/while/body/eval_jaxpr/kiat,kjbt->kabij/dot_general | solution.py:27
  526.0 5.6 copy.52
  536.3 5.4 convolution_convert_fusion.4
  541.7 6.9 reshape.110
  548.6 5.4 convolution_convert_fusion.5
  554.0 6.9 reshape.111
  560.9 12.5 %fusion.52 = f32[32,2,2,128,128]{3,4,1,2,0:T(8,128)S(1)} fusion(bf16[32,128,2,256,1]{3,2,0,1,4:T(2,128)(2,1)} %bitcast.152, bf16[32,128,2,256,1]{3,2,0,1,4:T(2,128)(2,1)} %bitcast.153), kind=kOutput, calls=%fused_computation.7.clone.1 | convolution fusion | flops 1073741824 | bytes 16777216 | tf_op jit(solution)/shard_map/while/body/eval_jaxpr/while/body/eval_jaxpr/kiat,kjbt->kabij/dot_general | solution.py:27
  576.3 5.6 copy.52
  581.9 4.7 constant_dynamic-update-slice_fusion.2
  586.6 5.4 convolution_convert_fusion.4
  592.1 6.9 reshape.110
  599.0 5.4 convolution_convert_fusion.5
  604.4 6.9 reshape.111
  611.3 12.5 %fusion.52 = f32[32,2,2,128,128]{3,4,1,2,0:T(8,128)S(1)} fusion(bf16[32,128,2,256,1]{3,2,0,1,4:T(2,128)(2,1)} %bitcast.152, bf16[32,128,2,256,1]{3,2,0,1,4:T(2,128)(2,1)} %bitcast.153), kind=kOutput, calls=%fused_computation.7.clone.1 | convolution fusion | flops 1073741824 | bytes 16777216 | tf_op jit(solution)/shard_map/while/body/eval_jaxpr/while/body/eval_jaxpr/kiat,kjbt->kabij/dot_general | solution.py:27
  626.7 5.6 copy.52
  637.0 5.4 convolution_convert_fusion.4
  642.4 6.9 reshape.110
  649.4 5.4 convolution_convert_fusion.5
  654.8 6.9 reshape.111
  661.7 12.5 %fusion.52 = f32[32,2,2,128,128]{3,4,1,2,0:T(8,128)S(1)} fusion(bf16[32,128,2,256,1]{3,2,0,1,4:T(2,128)(2,1)} %bitcast.152, bf16[32,128,2,256,1]{3,2,0,1,4:T(2,128)(2,1)} %bitcast.153), kind=kOutput, calls=%fused_computation.7.clone.1 | convolution fusion | flops 1073741824 | bytes 16777216 | tf_op jit(solution)/shard_map/while/body/eval_jaxpr/while/body/eval_jaxpr/kiat,kjbt->kabij/dot_general | solution.py:27
  677.1 5.6 copy.52
  682.7 4.7 constant_dynamic-update-slice_fusion.2
  687.4 11.6 %bitcast_dynamic-update-slice_fusion.2 = f32[2,128,2,128,128]{4,3,2,1,0:T(8,128)} fusion(f32[2,128,2,128,128]{4,3,2,1,0:T(8,128)} %get-tuple-element.207, s32[]{:T(128)} %get-tuple-element.206, f32[1,128,2,128,128]{4,3,2,1,0:T(8,128)} %bitcast.154), kind=kLoop, calls=%fused_computation.26.clone.1 | loop fusion | bytes 33554944 | tf_op jit(solution)/shard_map/while/body/jit(dynamic_update_index_in_dim)/dynamic_update_slice | solution.py:40
  699.0 19.9 %divide_convert_fusion = bf16[2,128,2,128,128]{4,3,2,1,0:T(8,128)(2,1)} fusion(f32[2,128,2,128,128]{4,3,2,1,0:T(8,128)} %get-tuple-element.58, f32[128,128,128]{2,1,0:T(8,128)} %multiply_sqrt_fusion), kind=kLoop, calls=%fused_computation.28 | loop fusion | flops 16777216 | bytes 58720256 | tf_op jit(solution)/shard_map/convert_element_type | solution.py:69
  (81 shorter events, 87.6 us)
Async XLA Ops:
  10.2 23.5 %copy-start = (bf16[256,32,512]{2,1,0:T(8,128)(2,1)S(1)}, bf16[256,32,512]{2,1,0:T(8,128)(2,1)}, u32[]{:S(2)}) copy-start(bf16[256,32,512]{2,1,0:T(8,128)(2,1)} %get-tuple-element.112) | copy-start | bytes 25165828
  44.7 199.5 %copy-start.1 = (s32[128,2]{0,1:T(2,128)S(1)}, s32[128,2]{0,1:T(2,128)}, u32[]{:S(2)}) copy-start(s32[128,2]{0,1:T(2,128)} %param.11) | copy-start | bytes 3076
  44.7 205.6 %all-to-all-start = ((bf16[16,256,2,512]{3,2,1,0:T(2,128)(2,1)}), bf16[16,256,2,512]{3,2,1,0:T(2,128)(2,1)}, u32[]{:S(2)}, u32[]{:S(2)}) async-start(bf16[16,256,2,512]{3,2,1,0:T(2,128)(2,1)} %fusion.19), calls=%async_computation | async-start | bytes 16777216 | tf_op jit(solution)/shard_map/all_to_all | solution.py:54
